TPU v7x, 32 devices: a whole 2x2x4 slice. The times are simulated.
32 devices in a mesh: row: 4 (over y, core), col: 8 (over z, x).
Axes of the slice: x: 2, y: 2, z: 4, core: 2. Of those that a mesh axis runs over, the one named last changes fastest.
Arguments:
- scatter_vectors: float32 [2, 2, 3, 128, 4096], P(None, None, None, 'row', 'col'), may hold values from -80 to 80
- ground_ratio: float32 [3], replicated, may hold values from 0.1 to 1
- vertical_wavenumber: float32 [128, 4096], P('row', 'col'), may hold values from 0.45 to 1.1
- initial_phase: float32 [128, 4096], P('row', 'col'), may hold values from 0.1 to 3.6
- initial_extinction: float32 [128, 4096], P('row', 'col'), may hold values from 0.1 to 2.9
Outputs:
- heights: float32 [128, 4096], P('row', 'col')
- extinction_depth: float32 [128, 4096], P('row', 'col')
All inputs are finite; a program needn't handle non-finite values.
Results may differ from a plain program's by a relative error of at most 0.00022.
Values sent between devices are 32-bit elements; how exact they have to be, the bound alone decides.
A program may use at most 64 MiB of HBM per device.

v0:
```python
import functools

import jax
import jax.numpy as jnp
from jax import lax
from jax.experimental import pallas as pl
from jax.experimental.pallas import tpu as pltpu
from jax.sharding import PartitionSpec as P

RADIUS = 9
LAYERS = 16
GAUSS_STEPS = 2
ITERS = 3

EPSILON = 1e-06
DAMPING = 0.002
SMOOTHING = 1.0

CHANNELS = 3
RAW = 4 * CHANNELS
GUESS = 3
GHOST = ITERS + 1
REACH = RADIUS + GHOST
SLOT = 16
LANES = 128
SHIFT = 4.5 * SMOOTHING
MESH = pl.DeviceIdType.MESH


def turn(value, amount, axis):
    size = value.shape[axis]
    amount = amount % size
    return value if amount == 0 else pltpu.roll(value, amount, axis)


def window(value, axis):
    pair = value + turn(value, -1, axis)
    four = pair + turn(pair, -2, axis)
    eight = four + turn(four, -4, axis)
    most = eight + turn(eight, -8, axis)
    return most + turn(pair, -16, axis) + turn(value, -18, axis)


def sine_cosine(angle):
    square = angle * angle
    sine = -1.0 / 39916800.0 + square * (1.0 / 6227020800.0)
    for term in (362880.0, -5040.0, 120.0, -6.0):
        sine = sine * square + 1.0 / term
    sine = angle + angle * square * sine
    cosine = -1.0 / 3628800.0 + square * (1.0 / 479001600.0)
    for term in (40320.0, -720.0, 24.0, -2.0):
        cosine = cosine * square + 1.0 / term
    return sine, 1.0 + square * cosine


def volume_moments(phase, atten):
    sin_half, cos_half = sine_cosine(phase * (0.5 / LAYERS))
    sin_n = 2.0 * sin_half * cos_half
    cos_n = 1.0 - 2.0 * sin_half * sin_half
    grown = jnp.exp(atten * (1.0 / LAYERS))
    weight = 1.0 + grown
    depth = grown
    step_r = grown * cos_n
    step_i = grown * sin_n
    sum_r = 1.0 + step_r
    sum_i = step_i
    deep_r = step_r
    deep_i = step_i
    count = 2
    while count < LAYERS:
        sin_n, cos_n = 2.0 * sin_n * cos_n, 1.0 - 2.0 * sin_n * sin_n
        grown = jnp.exp(atten * (float(count) / LAYERS))
        step_r = grown * cos_n
        step_i = grown * sin_n
        depth = depth + grown * (depth + float(count) * weight)
        weight = weight + grown * weight
        inner_r = deep_r + float(count) * sum_r
        inner_i = deep_i + float(count) * sum_i
        deep_r = deep_r + (step_r * inner_r - step_i * inner_i)
        deep_i = deep_i + (step_r * inner_i + step_i * inner_r)
        sum_r, sum_i = (
            sum_r + (step_r * sum_r - step_i * sum_i),
            sum_i + (step_r * sum_i + step_i * sum_r),
        )
        count *= 2
    scale = 1.0 / weight
    fine = scale * (1.0 / LAYERS)
    deep_r = deep_r + 0.5 * sum_r
    deep_i = deep_i + 0.5 * sum_i
    return (
        depth * fine + 0.5 / LAYERS,
        (cos_half * sum_r - sin_half * sum_i) * scale,
        (cos_half * sum_i + sin_half * sum_r) * scale,
        (cos_half * deep_r - sin_half * deep_i) * fine,
        (cos_half * deep_i + sin_half * deep_r) * fine,
    )


def gauss_newton(phase, atten, weighted_re, weighted_im, weight_total, offset_total):
    for _ in range(GAUSS_STEPS):
        mean, real, imag, depth_cos, depth_sin = volume_moments(phase, atten)
        ra = depth_cos - mean * real
        rt = -depth_sin
        ia = depth_sin - mean * imag
        it = depth_cos
        er = weighted_re - weight_total * real - offset_total
        ei = weighted_im - weight_total * imag
        maa = weight_total * (ra * ra + ia * ia) + DAMPING
        map_ = weight_total * (ra * rt + ia * it)
        mpp = weight_total * (rt * rt + it * it) + DAMPING
        ga = ra * er + ia * ei
        gp = rt * er + it * ei
        over = 1.0 / (maa * mpp - map_ * map_)
        atten = atten + (mpp * ga - map_ * gp) * over
        phase = phase + (maa * gp - map_ * ga) * over
    return phase, atten


def dot_poly(left, right, moments):
    total = None
    for i, a in enumerate(left):
        for j, b in enumerate(right):
            term = a * b * moments[i + j]
            total = term if total is None else total + term
    return total


def add_poly(left, right, scale):
    size = max(len(left), len(right))
    out = []
    for i in range(size):
        if i >= len(right):
            out.append(left[i])
        elif i >= len(left):
            out.append(scale * right[i])
        else:
            out.append(left[i] + scale * right[i])
    return out


def solve_coefficients(moments):
    one = jnp.ones_like(moments[0])
    residual = [one]
    direction = [one]
    answer = []
    norm = moments[0]
    for iteration in range(ITERS):
        image = [SHIFT * d for d in direction] + [0.0 * one]
        for i, d in enumerate(direction):
            image[i + 1] = image[i + 1] + d
        step = norm / dot_poly(direction, image, moments)
        answer = add_poly(answer, direction, step)
        if iteration + 1 < ITERS:
            residual = add_poly(residual, image, -step)
            following = dot_poly(residual, residual, moments)
            direction = add_poly(residual, direction, following / norm)
            norm = following
    return answer


def kernel(
    counts, ratio_in, vectors_in, wavenumber_in, phase_in, atten_in, heights, extinction,
    ratio, vectors, wavenumber, phase0, atten0, load_sem, row_send, row_recv, col_send, col_recv, corner_recv, fields, guess, sums,
    conf_buf, start_buf, mine, row_part, col_part,
    row_ss, row_rs, col_ss, col_rs, corner_ss, corner_rs, rsum_ss, rsum_rs, csum_ss, csum_rs,
):
    rows, cols = counts
    my_row = lax.axis_index("row")
    my_col = lax.axis_index("col")
    high, wide = phase0.shape
    full = wide + LANES
    tall = high + 2 * GHOST
    plain = (wavenumber, phase0, atten0)

    loads = [
        pltpu.make_async_copy(source, target, load_sem.at[i])
        for i, (source, target) in enumerate((
            (vectors_in, vectors), (wavenumber_in, wavenumber),
            (phase_in, phase0), (atten_in, atten0), (ratio_in, ratio),
        ))
    ]
    for load in loads:
        load.start()

    def row_peer(k):
        return lax.rem(my_row + k, rows)

    def col_peer(k):
        return lax.rem(my_col + k, cols)

    barrier = pltpu.get_barrier_semaphore()
    for k in range(1, rows):
        pl.semaphore_signal(barrier, inc=1, device_id=(row_peer(k), my_col), device_id_type=MESH)
    for k in range(1, cols):
        pl.semaphore_signal(barrier, inc=1, device_id=(my_row, col_peer(k)), device_id_type=MESH)

    has = (my_row > 0, my_row < rows - 1)
    beside = (my_col > 0, my_col < cols - 1)

    sent = row_send.shape[1]
    for side in (0, 1):
        row_recv[side, sent:, :] = jnp.zeros((row_recv.shape[1] - sent, wide), jnp.float32)
    first_row = GUESS * GHOST
    for load in loads:
        load.wait()
    for g in range(GUESS):
        row_send[0, g * GHOST : (g + 1) * GHOST, :] = plain[g][0:GHOST, :]
        row_send[1, g * GHOST : (g + 1) * GHOST, :] = plain[g][high - GHOST : high, :]
    for f in range(RAW):
        span = slice(first_row + f * REACH, first_row + (f + 1) * REACH)
        row_send[0, span, :] = vectors[f, 0:REACH, :]
        row_send[1, span, :] = vectors[f, high - REACH : high, :]

    def row_copy(side):
        return pltpu.make_async_remote_copy(
            src_ref=row_send.at[side],
            dst_ref=row_recv.at[1 - side, 0:sent, :],
            send_sem=row_ss.at[side],
            recv_sem=row_rs.at[1 - side],
            device_id=(my_row - 1 + 2 * side, my_col),
            device_id_type=MESH,
        )

    def col_copy(side):
        return pltpu.make_async_remote_copy(
            src_ref=col_send.at[side],
            dst_ref=col_recv.at[1 - side],
            send_sem=col_ss.at[side],
            recv_sem=col_rs.at[1 - side],
            device_id=(my_row, my_col - 1 + 2 * side),
            device_id_type=MESH,
        )

    def corner_copy(side):
        begin = 0 if side == 0 else high - SLOT
        return pltpu.make_async_remote_copy(
            src_ref=col_recv.at[:, begin : begin + SLOT, :],
            dst_ref=corner_recv.at[1 - side],
            send_sem=corner_ss.at[side],
            recv_sem=corner_rs.at[1 - side],
            device_id=(my_row - 1 + 2 * side, my_col),
            device_id_type=MESH,
        )

    pl.semaphore_wait(barrier, rows + cols - 2)
    for side in (0, 1):
        pl.when(has[side])(lambda side=side: row_copy(side).start())

    lane = lax.broadcasted_iota(jnp.int32, (high, LANES), 1)
    per = LANES // SLOT
    packs = (RAW + GUESS + per - 1) // per
    for k in range(packs):
        low = jnp.zeros((high, LANES), jnp.float32)
        top = jnp.zeros((high, LANES), jnp.float32)
        for p in range(per):
            f = k * per + p
            if f >= RAW + GUESS:
                continue
            if f < RAW:
                first, last = vectors[f, :, 0:LANES], vectors[f, :, wide - LANES : wide]
            else:
                ref = plain[f - RAW]
                first, last = ref[:, 0:LANES], ref[:, wide - LANES : wide]
            here = (lane >= p * SLOT) & (lane < (p + 1) * SLOT)
            low = jnp.where(here, turn(first, p * SLOT, 1), low)
            top = jnp.where(here, turn(last, (p + 1) * SLOT, 1), top)
        col_send[0, :, k * LANES : (k + 1) * LANES] = low
        col_send[1, :, k * LANES : (k + 1) * LANES] = top

    for side in (0, 1):
        pl.when(beside[side])(lambda side=side: col_copy(side).start())

    for side in (0, 1):
        @pl.when(jnp.logical_not(has[side]))
        def _(side=side):
            row_recv[side] = jnp.zeros(row_recv.shape[1:], jnp.float32)
            corner_recv[side] = jnp.zeros(corner_recv.shape[1:], jnp.float32)

        @pl.when(jnp.logical_not(beside[side]))
        def _(side=side):
            col_recv[side] = jnp.zeros(col_recv.shape[1:], jnp.float32)

    def products(raws):
        re1, im1, re2, im2 = raws
        return (
            re1 * re1 + im1 * im1,
            re2 * re2 + im2 * im2,
            re1 * re2 + im1 * im2,
            re1 * im2 - im1 * re2,
        )

    deep = -(-(2 * REACH + high) // 8) * 8
    above_own = jnp.zeros((REACH, LANES), jnp.float32)
    below_own = jnp.zeros((deep - REACH - high, LANES), jnp.float32)

    def own_sums(channel, raws, piece):
        for i, product in enumerate(products(raws)):
            placed = jnp.concatenate([above_own, product, below_own], axis=0)
            sums[4 * channel + i, :, piece] = window(placed, 0)[0:tall, :]

    def inner_sums(channel, carry):
        for strip in range(wide // LANES):
            piece = slice(strip * LANES, (strip + 1) * LANES)
            own_sums(channel, [vectors[CHANNELS * i + channel, :, piece] for i in range(4)], piece)
        return carry

    lax.fori_loop(0, CHANNELS, inner_sums, 0)
    for g in range(GUESS):
        guess[g, GHOST : GHOST + high, 0:wide] = plain[g][...]

    for side in (0, 1):
        pl.when(beside[side])(lambda side=side: col_copy(1 - side).wait_recv())
    for side in (0, 1):
        pl.when(has[side])(lambda side=side: corner_copy(side).start())

    def unpacked(left, right, f):
        p = f % per
        place = lax.broadcasted_iota(jnp.int32, left.shape, 1)
        return jnp.where(
            place < LANES // 2,
            turn(right, -p * SLOT, 1),
            turn(left, LANES - SLOT - p * SLOT, 1),
        )

    def outer(f):
        piece = slice(f // per * LANES, (f // per + 1) * LANES)
        return unpacked(col_recv[0, :, piece], col_recv[1, :, piece], f)

    for channel in range(CHANNELS):
        own_sums(channel, [outer(CHANNELS * i + channel) for i in range(4)], slice(wide, full))
    for g in range(GUESS):
        guess[g, GHOST : GHOST + high, wide:full] = outer(RAW + g)

    ratios = [jnp.full((1, full), ratio[k], jnp.float32) for k in range(CHANNELS)]
    weights = [1.0 / (1.0 + r) for r in ratios]
    weight_total = sum(w * w for w in weights)
    offset_total = sum(r * w * w for r, w in zip(ratios, weights))

    def fit(chunk):
        block = pl.ds(pl.multiple_of(chunk * 8, 8), 8)
        found = None
        for k in range(CHANNELS):
            power1, power2, cross_re, cross_im = [
                window(sums[4 * k + i, block, :], 1) for i in range(4)
            ]
            scale = lax.rsqrt(power1 * power2 + EPSILON)
            real = cross_re * scale
            imag = cross_im * scale
            parts = (real * weights[k], imag * weights[k], real * real + imag * imag)
            found = parts if k == 0 else [a + b for a, b in zip(found, parts)]
        weighted_re, weighted_im, confidence = [turn(a, RADIUS, 1) for a in found]
        phase, atten = gauss_newton(
            guess[1, block, :], guess[2, block, :], weighted_re, weighted_im,
            weight_total, offset_total,
        )
        conf_buf[block, :] = confidence * (1.0 / CHANNELS)
        start_buf[0, block, :] = phase / guess[0, block, :]
        start_buf[1, block, :] = atten

    chunks = tall // 8
    edge_chunks = SLOT // 8

    def middle(chunk, carry):
        fit(chunk)
        return carry

    lax.fori_loop(edge_chunks, chunks - edge_chunks, middle, 0)

    for side in (0, 1):
        @pl.when(has[side])
        def _(side=side):
            row_copy(1 - side).wait_recv()
            corner_copy(1 - side).wait_recv()

    line = lax.broadcasted_iota(jnp.int32, (SLOT, LANES), 0)
    keep = (line < REACH, line >= SLOT - REACH)

    def running(value, down):
        for k in (1, 2, 4, 8):
            if down:
                value = value + jnp.where(line >= k, turn(value, k, 0), 0.0)
            else:
                value = value + jnp.where(line < SLOT - k, turn(value, -k, 0), 0.0)
        return value

    def corner(side, f):
        piece = slice(f // per * LANES, (f // per + 1) * LANES)
        return unpacked(corner_recv[side, 0, :, piece], corner_recv[side, 1, :, piece], f)

    def halo_rows(side, f, strip):
        if strip < wide // LANES:
            begin = first_row + f * REACH - side * (SLOT - REACH)
            value = row_recv[side, begin : begin + SLOT, strip * LANES : (strip + 1) * LANES]
        else:
            value = turn(corner(side, f), (1 - 2 * side) * (REACH - SLOT), 0)
        return jnp.where(keep[side], value, 0.0)

    for side in (0, 1):
        begin = side * (tall - SLOT)
        for channel in range(CHANNELS):
            for strip in range(full // LANES):
                piece = slice(strip * LANES, (strip + 1) * LANES)
                raws = [halo_rows(side, CHANNELS * i + channel, strip) for i in range(4)]
                for i, product in enumerate(products(raws)):
                    sums[4 * channel + i, begin : begin + SLOT, piece] += running(product, side == 1)
    for g in range(GUESS):
        span = slice(g * GHOST, (g + 1) * GHOST)
        guess[g, 0:GHOST, 0:wide] = row_recv[0, span, :]
        guess[g, GHOST + high : tall, 0:wide] = row_recv[1, span, :]
        guess[g, 0:GHOST, wide:full] = corner(0, RAW + g)[SLOT - GHOST :, :]
        guess[g, GHOST + high : tall, wide:full] = corner(1, RAW + g)[0:GHOST, :]

    def edges(step, carry):
        fit(step + step // edge_chunks * (chunks - 2 * edge_chunks))
        return carry

    lax.fori_loop(0, 2 * edge_chunks, edges, 0)

    row_at = lax.broadcasted_iota(jnp.int32, (tall, full), 0) - GHOST
    lane_at = lax.broadcasted_iota(jnp.int32, (tall, full), 1)
    col_at = jnp.where(lane_at < wide + LANES // 2, lane_at, lane_at - full)
    near = (col_at >= -GHOST) & (col_at < wide + GHOST)
    row_all = row_at + my_row * high
    col_all = col_at + my_col * wide
    inside = near & (row_all >= 0) & (row_all < rows * high) & (col_all >= 0) & (col_all < cols * wide)

    def masked(value):
        return jnp.where(inside, value, 0.0)

    def around(value):
        return turn(value, 1, 0) + turn(value, -1, 0) + turn(value, 1, 1) + turn(value, -1, 1)

    start = masked(start_buf[0])
    confidence = conf_buf[...]
    centred = confidence + (4.0 * SMOOTHING - SHIFT)
    basis = [masked(SMOOTHING * (around(start) - 4.0 * start))]
    for _ in range(ITERS - 1):
        basis.append(masked(centred * basis[-1] - SMOOTHING * around(basis[-1])))
    basis.append(centred * basis[-1] - SMOOTHING * around(basis[-1]))

    extinction[...] = start_buf[1, GHOST : GHOST + high, 0:wide]
    own = inside & (row_at >= 0) & (row_at < high) & (lane_at < wide)
    for m in range(2 * ITERS):
        product = jnp.where(own, basis[m // 2] * basis[m - m // 2], 0.0)
        line = jnp.sum(product, axis=0, keepdims=True)
        total = line[:, 0:LANES]
        for strip in range(1, wide // LANES):
            total = total + line[:, strip * LANES : (strip + 1) * LANES]
        mine[m : m + 1, :] = total
    mine[2 * ITERS :, :] = jnp.zeros((8 - 2 * ITERS, LANES), jnp.float32)
    start_buf[0] = start
    for i in range(ITERS):
        fields[i] = basis[i]

    def row_share(k):
        return pltpu.make_async_remote_copy(
            src_ref=mine,
            dst_ref=row_part.at[my_row],
            send_sem=rsum_ss.at[k],
            recv_sem=rsum_rs.at[my_row],
            device_id=(row_peer(k), my_col),
            device_id_type=MESH,
        )

    def row_arrival(k):
        who = row_peer(k)
        return pltpu.make_async_remote_copy(
            src_ref=mine,
            dst_ref=row_part.at[who],
            send_sem=rsum_ss.at[k],
            recv_sem=rsum_rs.at[who],
            device_id=(who, my_col),
            device_id_type=MESH,
        )

    for k in range(1, rows):
        row_share(k).start()
    row_part[my_row] = mine[...]
    for k in range(1, rows):
        row_arrival(k).wait_recv()
    strip_sum = row_part[0]
    for k in range(1, rows):
        strip_sum = strip_sum + row_part[k]
    col_part[my_col] = strip_sum

    def col_share(k, slot):
        return pltpu.make_async_remote_copy(
            src_ref=col_part.at[my_col],
            dst_ref=col_part.at[slot],
            send_sem=csum_ss.at[k],
            recv_sem=csum_rs.at[slot],
            device_id=(my_row, col_peer(k)),
            device_id_type=MESH,
        )

    for k in range(1, cols):
        col_share(k, my_col).start()
    for k in range(1, cols):
        col_share(k, col_peer(k)).wait_recv()
    everything = col_part[0]
    for k in range(1, cols):
        everything = everything + col_part[k]
    everything = jnp.sum(everything, axis=1, keepdims=True)
    moments = [everything[m : m + 1, :] for m in range(2 * ITERS)]
    answer = solve_coefficients(moments)
    result = start_buf[0, GHOST : GHOST + high, 0:wide]
    for i, scale in enumerate(answer):
        result = result + scale * fields[i, GHOST : GHOST + high, 0:wide]
    heights[...] = result

    for side in (0, 1):
        @pl.when(has[side])
        def _(side=side):
            row_copy(side).wait_send()
            corner_copy(side).wait_send()

        pl.when(beside[side])(lambda side=side: col_copy(side).wait_send())
    for k in range(1, rows):
        row_share(k).wait_send()
    for k in range(1, cols):
        col_share(k, my_col).wait_send()


def local(counts, scatter_vectors, ground_ratio, vertical_wavenumber, initial_phase, initial_extinction):
    high, wide = initial_phase.shape
    rows, cols = counts
    vectors = scatter_vectors.reshape(RAW, high, wide)
    full = wide + LANES
    tall = high + 2 * GHOST
    edge = -(-(RAW * REACH + GUESS * GHOST) // 8) * 8
    packed = -(-(RAW + GUESS) * SLOT // LANES) * LANES
    vmem = pl.BlockSpec(memory_space=pltpu.VMEM)
    f32 = jnp.float32
    dma = pltpu.SemaphoreType.DMA
    out = jax.ShapeDtypeStruct((high, wide), f32)
    heights, extinction = pl.pallas_call(
        functools.partial(kernel, counts),
        out_shape=(out, out),
        in_specs=[pl.BlockSpec(memory_space=pltpu.HBM)] * 5,
        out_specs=(vmem, vmem),
        scratch_shapes=[
            pltpu.SMEM((CHANNELS,), f32),
            pltpu.VMEM((RAW, high, wide), f32),
            pltpu.VMEM((high, wide), f32),
            pltpu.VMEM((high, wide), f32),
            pltpu.VMEM((high, wide), f32),
            dma((5,)),
            pltpu.VMEM((2, edge, wide), f32),
            pltpu.VMEM((2, edge + 8, wide), f32),
            pltpu.VMEM((2, high, packed), f32),
            pltpu.VMEM((2, high, packed), f32),
            pltpu.VMEM((2, 2, SLOT, packed), f32),
            pltpu.VMEM((ITERS, tall, full), f32),
            pltpu.VMEM((GUESS, tall, full), f32),
            pltpu.VMEM((RAW, tall, full), f32),
            pltpu.VMEM((tall, full), f32),
            pltpu.VMEM((2, tall, full), f32),
            pltpu.VMEM((8, LANES), f32),
            pltpu.VMEM((rows, 8, LANES), f32),
            pltpu.VMEM((cols, 8, LANES), f32),
            dma((2,)), dma((2,)), dma((2,)), dma((2,)), dma((2,)), dma((2,)),
            dma((rows,)), dma((rows,)), dma((cols,)), dma((cols,)),
        ],
        compiler_params=pltpu.CompilerParams(
            collective_id=0, has_side_effects=True, vmem_limit_bytes=32 * 1024 * 1024
        ),
        cost_estimate=pl.CostEstimate(
            flops=2000 * high * wide, bytes_accessed=80 * high * wide, transcendentals=8 * high * wide
        ),
    )(ground_ratio, vectors, vertical_wavenumber, initial_phase, initial_extinction)
    return (heights, extinction)


def solution(mesh):
    placed = (
        P(None, None, None, "row", "col"),
        P(),
        P("row", "col"),
        P("row", "col"),
        P("row", "col"),
    )
    counts = (mesh.shape["row"], mesh.shape["col"])
    return jax.shard_map(
        functools.partial(local, counts),
        mesh=mesh,
        in_specs=placed,
        out_specs=(P("row", "col"), P("row", "col")),
        check_vma=False,
    )
```

profile of v0, /device:TPU:0, one launch (start us, length us, event | category | flops | bytes accessed | tf_op | source)
XLA Modules:
  0.0 29.7 jit_solution(3397627163969128049)
XLA Ops:
  0.6 0.0 copy-start.4
  0.6 0.6 %copy-done.4 = f32[3]{0:T(128)S(1)} copy-done((f32[3]{0:T(128)S(1)}, f32[3]{0:T(128)}, u32[]{:S(2)}) %copy-start.4) | copy-done | bytes 36
  1.3 0.0 copy-start
  1.3 1.1 %copy-done = f32[2,2,3,32,512]{4,3,2,1,0:T(8,128)S(1)} copy-done((f32[2,2,3,32,512]{4,3,2,1,0:T(8,128)S(1)}, f32[2,2,3,32,512]{4,3,2,1,0:T(8,128)}, u32[]{:S(2)}) %copy-start) | copy-done | bytes 786456
  2.4 0.0 copy-start.1
  2.4 0.8 %copy-done.1 = f32[32,512]{1,0:T(8,128)S(1)} copy-done((f32[32,512]{1,0:T(8,128)S(1)}, f32[32,512]{1,0:T(8,128)}, u32[]{:S(2)}) %copy-start.1) | copy-done | bytes 65560
  3.3 0.0 copy-start.2
  3.3 0.8 %copy-done.2 = f32[32,512]{1,0:T(8,128)S(1)} copy-done((f32[32,512]{1,0:T(8,128)S(1)}, f32[32,512]{1,0:T(8,128)}, u32[]{:S(2)}) %copy-start.2) | copy-done | bytes 65560
  4.1 0.0 copy-start.3
  4.1 0.8 %copy-done.3 = f32[32,512]{1,0:T(8,128)S(1)} copy-done((f32[32,512]{1,0:T(8,128)S(1)}, f32[32,512]{1,0:T(8,128)}, u32[]{:S(2)}) %copy-start.3) | copy-done | bytes 65560
  4.9 23.4 %shard_map.68 = (f32[32,512]{1,0:T(8,128)S(1)}, f32[32,512]{1,0:T(8,128)S(1)}) custom-call(f32[3]{0:T(128)S(1)} %copy-done.4, f32[12,32,512]{2,1,0:T(8,128)S(1)} %bitcast.1, f32[32,512]{1,0:T(8,128)S(1)} %copy-done.1, f32[32,512]{1,0:T(8,128)S(1)} %copy-done.2, f32[32,512]{1,0:T(8,128)S(1)} %copy-done.3), custom_call_target="tpu_custom_call" | custom-call | flops 32768000 | bytes 1310720 | tf_op jit(solution)/shard_map/pallas_call | solution.py:536
  28.4 0.6 %copy.9 = f32[32,512]{1,0:T(8,128)} copy(f32[32,512]{1,0:T(8,128)S(1)} %get-tuple-element.4) | data formatting | bytes 131072
  29.0 0.6 %copy.10 = f32[32,512]{1,0:T(8,128)} copy(f32[32,512]{1,0:T(8,128)S(1)} %get-tuple-element.5) | data formatting | bytes 131072
Async XLA Ops:
  0.6 0.7 %copy-start.4 = (f32[3]{0:T(128)S(1)}, f32[3]{0:T(128)}, u32[]{:S(2)}) copy-start(f32[3]{0:T(128)} %ratio_in.1) | copy-start | bytes 40
  1.3 1.1 %copy-start = (f32[2,2,3,32,512]{4,3,2,1,0:T(8,128)S(1)}, f32[2,2,3,32,512]{4,3,2,1,0:T(8,128)}, u32[]{:S(2)}) copy-start(f32[2,2,3,32,512]{4,3,2,1,0:T(8,128)} %param.5) | copy-start | bytes 2359300
  2.4 0.8 %copy-start.1 = (f32[32,512]{1,0:T(8,128)S(1)}, f32[32,512]{1,0:T(8,128)}, u32[]{:S(2)}) copy-start(f32[32,512]{1,0:T(8,128)} %wavenumber_in.1) | copy-start | bytes 196612
  3.3 0.8 %copy-start.2 = (f32[32,512]{1,0:T(8,128)S(1)}, f32[32,512]{1,0:T(8,128)}, u32[]{:S(2)}) copy-start(f32[32,512]{1,0:T(8,128)} %phase_in.1) | copy-start | bytes 196612
  4.1 0.8 %copy-start.3 = (f32[32,512]{1,0:T(8,128)S(1)}, f32[32,512]{1,0:T(8,128)}, u32[]{:S(2)}) copy-start(f32[32,512]{1,0:T(8,128)} %atten_in.1) | copy-start | bytes 196612
where the time goes:
time: 30 us; the launch traced here: 29.7 us
  Pallas kernels  23.4 us (78%)
  local copies, waits for them, and re-layouts  5.56 us (19%)
  between operations  0.65 us (2%)
    pallas_call x1, Pallas kernels, local(): pl.pallas_call(functools.partial(kernel, counts), out_shape=(out, out), i...  23.4 us
    unnamed x12, local copies, waits for them, and re-layouts  5.56 us

commit v1 on v0

--- a/solution.py
+++ b/solution.py
@@ -96,9 +96,11 @@
     )
 
 
-def gauss_newton(phase, atten, weighted_re, weighted_im, weight_total, offset_total):
-    for _ in range(GAUSS_STEPS):
-        mean, real, imag, depth_cos, depth_sin = volume_moments(phase, atten)
+def gauss_newton(phase, atten, known, weighted_re, weighted_im, weight_total, offset_total):
+    for step in range(GAUSS_STEPS):
+        if step > 0:
+            known = volume_moments(phase, atten)
+        mean, real, imag, depth_cos, depth_sin = known
         ra = depth_cos - mean * real
         rt = -depth_sin
         ia = depth_sin - mean * imag
@@ -159,8 +161,8 @@
 
 
 def kernel(
-    counts, ratio_in, vectors_in, wavenumber_in, phase_in, atten_in, heights, extinction,
-    ratio, vectors, wavenumber, phase0, atten0, load_sem, row_send, row_recv, col_send, col_recv, corner_recv, fields, guess, sums,
+    counts, ratio_in, vectors_in, wavenumber_in, phase_in, atten_in, parts_out, answer_out,
+    ratio, vectors, wavenumber, phase0, atten0, load_sem, store_sem, parts, first_fit, row_send, row_recv, col_send, col_recv, corner_recv, guess, sums,
     conf_buf, start_buf, mine, row_part, col_part,
     row_ss, row_rs, col_ss, col_rs, corner_ss, corner_rs, rsum_ss, rsum_rs, csum_ss, csum_rs,
 ):
@@ -350,13 +352,23 @@
             found = parts if k == 0 else [a + b for a, b in zip(found, parts)]
         weighted_re, weighted_im, confidence = [turn(a, RADIUS, 1) for a in found]
         phase, atten = gauss_newton(
-            guess[1, block, :], guess[2, block, :], weighted_re, weighted_im,
-            weight_total, offset_total,
+            guess[1, block, :], guess[2, block, :], [first_fit[i, block, :] for i in range(5)],
+            weighted_re, weighted_im, weight_total, offset_total,
         )
         conf_buf[block, :] = confidence * (1.0 / CHANNELS)
         start_buf[0, block, :] = phase / guess[0, block, :]
         start_buf[1, block, :] = atten
 
+    for g in range(GUESS):
+        guess[g, 0:GHOST, :] = jnp.zeros((GHOST, full), jnp.float32)
+        guess[g, GHOST + high : tall, :] = jnp.zeros((GHOST, full), jnp.float32)
+
+    def guessed(chunk, carry):
+        block = pl.ds(pl.multiple_of(chunk * 8, 8), 8)
+        for i, moment in enumerate(volume_moments(guess[1, block, :], guess[2, block, :])):
+            first_fit[i, block, :] = moment
+        return carry
+
     chunks = tall // 8
     edge_chunks = SLOT // 8
 
@@ -364,6 +376,7 @@
         fit(chunk)
         return carry
 
+    lax.fori_loop(0, chunks, guessed, 0)
     lax.fori_loop(edge_chunks, chunks - edge_chunks, middle, 0)
 
     for side in (0, 1):
@@ -410,6 +423,13 @@
         guess[g, 0:GHOST, wide:full] = corner(0, RAW + g)[SLOT - GHOST :, :]
         guess[g, GHOST + high : tall, wide:full] = corner(1, RAW + g)[0:GHOST, :]
 
+    ghosts = [
+        jnp.concatenate([guess[g, 0:GHOST, :], guess[g, GHOST + high : tall, :]], axis=0) for g in (1, 2)
+    ]
+    for i, moment in enumerate(volume_moments(*ghosts)):
+        first_fit[i, 0:GHOST, :] = moment[0:GHOST, :]
+        first_fit[i, GHOST + high : tall, :] = moment[GHOST : 2 * GHOST, :]
+
     def edges(step, carry):
         fit(step + step // edge_chunks * (chunks - 2 * edge_chunks))
         return carry
@@ -438,7 +458,11 @@
         basis.append(masked(centred * basis[-1] - SMOOTHING * around(basis[-1])))
     basis.append(centred * basis[-1] - SMOOTHING * around(basis[-1]))
 
-    extinction[...] = start_buf[1, GHOST : GHOST + high, 0:wide]
+    parts[0] = start[GHOST : GHOST + high, 0:wide]
+    for i in range(ITERS):
+        parts[1 + i] = basis[i][GHOST : GHOST + high, 0:wide]
+    parts[1 + ITERS] = start_buf[1, GHOST : GHOST + high, 0:wide]
+    store = pltpu.make_async_copy(parts, parts_out, store_sem)
     own = inside & (row_at >= 0) & (row_at < high) & (lane_at < wide)
     for m in range(2 * ITERS):
         product = jnp.where(own, basis[m // 2] * basis[m - m // 2], 0.0)
@@ -448,9 +472,6 @@
             total = total + line[:, strip * LANES : (strip + 1) * LANES]
         mine[m : m + 1, :] = total
     mine[2 * ITERS :, :] = jnp.zeros((8 - 2 * ITERS, LANES), jnp.float32)
-    start_buf[0] = start
-    for i in range(ITERS):
-        fields[i] = basis[i]
 
     def row_share(k):
         return pltpu.make_async_remote_copy(
@@ -475,6 +496,7 @@
 
     for k in range(1, rows):
         row_share(k).start()
+    store.start()
     row_part[my_row] = mine[...]
     for k in range(1, rows):
         row_arrival(k).wait_recv()
@@ -503,10 +525,10 @@
     everything = jnp.sum(everything, axis=1, keepdims=True)
     moments = [everything[m : m + 1, :] for m in range(2 * ITERS)]
     answer = solve_coefficients(moments)
-    result = start_buf[0, GHOST : GHOST + high, 0:wide]
     for i, scale in enumerate(answer):
-        result = result + scale * fields[i, GHOST : GHOST + high, 0:wide]
-    heights[...] = result
+        answer_out[i : i + 1, :] = jnp.broadcast_to(scale, (1, wide))
+    answer_out[ITERS:, :] = jnp.zeros((8 - ITERS, wide), jnp.float32)
+    store.wait()
 
     for side in (0, 1):
         @pl.when(has[side])
@@ -532,12 +554,15 @@
     vmem = pl.BlockSpec(memory_space=pltpu.VMEM)
     f32 = jnp.float32
     dma = pltpu.SemaphoreType.DMA
-    out = jax.ShapeDtypeStruct((high, wide), f32)
-    heights, extinction = pl.pallas_call(
+    out = (
+        jax.ShapeDtypeStruct((2 + ITERS, high, wide), f32),
+        jax.ShapeDtypeStruct((8, wide), f32),
+    )
+    parts, answer = pl.pallas_call(
         functools.partial(kernel, counts),
-        out_shape=(out, out),
+        out_shape=out,
         in_specs=[pl.BlockSpec(memory_space=pltpu.HBM)] * 5,
-        out_specs=(vmem, vmem),
+        out_specs=(pl.BlockSpec(memory_space=pltpu.HBM), vmem),
         scratch_shapes=[
             pltpu.SMEM((CHANNELS,), f32),
             pltpu.VMEM((RAW, high, wide), f32),
@@ -545,12 +570,14 @@
             pltpu.VMEM((high, wide), f32),
             pltpu.VMEM((high, wide), f32),
             dma((5,)),
+            dma(()),
+            pltpu.VMEM((2 + ITERS, high, wide), f32),
+            pltpu.VMEM((5, tall, full), f32),
             pltpu.VMEM((2, edge, wide), f32),
             pltpu.VMEM((2, edge + 8, wide), f32),
             pltpu.VMEM((2, high, packed), f32),
             pltpu.VMEM((2, high, packed), f32),
             pltpu.VMEM((2, 2, SLOT, packed), f32),
-            pltpu.VMEM((ITERS, tall, full), f32),
             pltpu.VMEM((GUESS, tall, full), f32),
             pltpu.VMEM((RAW, tall, full), f32),
             pltpu.VMEM((tall, full), f32),
@@ -562,13 +589,16 @@
             dma((rows,)), dma((rows,)), dma((cols,)), dma((cols,)),
         ],
         compiler_params=pltpu.CompilerParams(
-            collective_id=0, has_side_effects=True, vmem_limit_bytes=32 * 1024 * 1024
+            collective_id=0, has_side_effects=True, vmem_limit_bytes=56 * 1024 * 1024
         ),
         cost_estimate=pl.CostEstimate(
             flops=2000 * high * wide, bytes_accessed=80 * high * wide, transcendentals=8 * high * wide
         ),
     )(ground_ratio, vectors, vertical_wavenumber, initial_phase, initial_extinction)
-    return (heights, extinction)
+    heights = parts[0]
+    for i in range(ITERS):
+        heights = heights + answer[i : i + 1, :] * parts[1 + i]
+    return (heights, parts[1 + ITERS])
 
 
 def solution(mesh):

time: 30 us -> 28.6 us (0.953)
  local copies, waits for them, and re-layouts: 5.56 us -> 2.31 us
  other arithmetic: 0 us -> 1.59 us
  Pallas kernels: 23.4 us -> 23.7 us
    unnamed x12 -> x0, local copies, waits for them, and re-layouts: 5.56 us -> none
    add x0 -> x1, other arithmetic: none -> 1.59 us  [local(): heights = heights + answer[i:i + 1, :] * parts[1 + i]]
    squeeze x0 -> x1, local copies, waits for them, and re-layouts: none -> 1.47 us  [local(): return (heights, parts[1 + ITERS])]
    slice x0 -> x1, local copies, waits for them, and re-layouts: none -> 0.84 us  [local(): heights = heights + answer[i:i + 1, :] * parts[1 + i]]
    pallas_call x1, Pallas kernels: 23.4 us -> 23.7 us  [local(): pl.pallas_call(functools.partial(kernel, counts), out_shape=out, in_specs...]
where the time goes in v1:
time: 28.6 us; the launch traced here: 28.3 us
  Pallas kernels  23.7 us (83%)
  local copies, waits for them, and re-layouts  2.31 us (8%)
  other arithmetic  1.59 us (6%)
  between operations  0.64 us (2%)
    pallas_call x1, Pallas kernels, local(): pl.pallas_call(functools.partial(kernel, counts), out_shape=out, in_specs...  23.7 us
    add x1, other arithmetic, local(): heights = heights + answer[i:i + 1, :] * parts[1 + i]  1.59 us
    squeeze x1, local copies, waits for them, and re-layouts, local(): return (heights, parts[1 + ITERS])  1.47 us
    slice x1, local copies, waits for them, and re-layouts, local(): heights = heights + answer[i:i + 1, :] * parts[1 + i]  0.84 us

profile of v1, /device:TPU:0, one launch (start us, length us, event | category | flops | bytes accessed | tf_op | source)
XLA Modules:
  0.0 28.3 jit_solution(1163393578404070943)
XLA Ops:
  0.6 23.7 %shard_map.68 = (f32[5,32,512]{2,1,0:T(8,128)}, f32[8,512]{1,0:T(8,128)}) custom-call(f32[3]{0:T(128)} %ratio_in.1, f32[12,32,512]{2,1,0:T(8,128)} %bitcast.24, f32[32,512]{1,0:T(8,128)} %wavenumber_in.1, f32[32,512]{1,0:T(8,128)} %phase_in.1, f32[32,512]{1,0:T(8,128)} %atten_in.1), custom_call_target="tpu_custom_call" | custom-call | flops 32768000 | bytes 1310720 | tf_op jit(solution)/shard_map/pallas_call | solution.py:561
  24.4 0.8 %fusion.3 = (f32[1,512]{1,0:T(1,128)S(1)}, f32[1,512]{1,0:T(1,128)S(1)}, f32[1,512]{1,0:T(1,128)S(1)}) fusion(f32[8,512]{1,0:T(8,128)} %get-tuple-element.5), kind=kLoop, calls=%fused_computation.7 | loop fusion | bytes 12288 | tf_op jit(solution)/shard_map/slice | solution.py:600
  25.2 1.6 %fusion = f32[32,512]{1,0:T(8,128)} fusion(f32[5,32,512]{2,1,0:T(8,128)} %get-tuple-element.4, f32[512]{0:T(512)S(1)} %bitcast.26, f32[512]{0:T(512)S(1)} %bitcast.27, f32[512]{0:T(512)S(1)} %bitcast.25), kind=kLoop, calls=%fused_computation.1 | loop fusion | flops 98304 | bytes 333824 | tf_op jit(solution)/shard_map/add | solution.py:600
  26.8 1.5 %slice_bitcast_fusion = f32[32,512]{1,0:T(8,128)} fusion(f32[5,32,512]{2,1,0:T(8,128)} %get-tuple-element.4), kind=kLoop, calls=%fused_computation.6 | loop fusion | bytes 131072 | tf_op jit(solution)/shard_map/squeeze | solution.py:601

commit v2 on v1

--- a/solution.py
+++ b/solution.py
@@ -161,8 +161,8 @@
 
 
 def kernel(
-    counts, ratio_in, vectors_in, wavenumber_in, phase_in, atten_in, parts_out, answer_out,
-    ratio, vectors, wavenumber, phase0, atten0, load_sem, store_sem, parts, first_fit, row_send, row_recv, col_send, col_recv, corner_recv, guess, sums,
+    counts, edges_at, ratio_in, vectors_in, wavenumber_in, phase_in, atten_in, parts_out,
+    ratio, vectors, wavenumber, phase0, atten0, load_sem, store_sem, results, mixed, parts, first_fit, row_send, row_recv, col_send, col_recv, corner_recv, guess, sums,
     conf_buf, start_buf, mine, row_part, col_part,
     row_ss, row_rs, col_ss, col_rs, corner_ss, corner_rs, rsum_ss, rsum_rs, csum_ss, csum_rs,
 ):
@@ -199,26 +199,40 @@
     has = (my_row > 0, my_row < rows - 1)
     beside = (my_col > 0, my_col < cols - 1)
 
-    sent = row_send.shape[1]
     for side in (0, 1):
-        row_recv[side, sent:, :] = jnp.zeros((row_recv.shape[1] - sent, wide), jnp.float32)
-    first_row = GUESS * GHOST
+        for channel in range(CHANNELS):
+            used = edges_at[channel] + 4 * REACH + (GUESS * GHOST if channel == 0 else 0)
+            if used < edges_at[channel + 1]:
+                spare = edges_at[channel + 1] - used
+                row_send[side, used : edges_at[channel + 1], :] = jnp.zeros((spare, wide), jnp.float32)
+
+    lead = (GUESS - 1) * GHOST
+
+    def row_begin(f):
+        channel, i = f % CHANNELS, f // CHANNELS
+        return edges_at[channel] + (lead if channel == 0 else 0) + i * REACH
+
+    def guess_rows(g):
+        begin = g * GHOST if g < GUESS - 1 else lead + 4 * REACH
+        return slice(begin, begin + GHOST)
+
     for load in loads:
         load.wait()
     for g in range(GUESS):
-        row_send[0, g * GHOST : (g + 1) * GHOST, :] = plain[g][0:GHOST, :]
-        row_send[1, g * GHOST : (g + 1) * GHOST, :] = plain[g][high - GHOST : high, :]
+        row_send[0, guess_rows(g), :] = plain[g][0:GHOST, :]
+        row_send[1, guess_rows(g), :] = plain[g][high - GHOST : high, :]
     for f in range(RAW):
-        span = slice(first_row + f * REACH, first_row + (f + 1) * REACH)
+        span = slice(row_begin(f), row_begin(f) + REACH)
         row_send[0, span, :] = vectors[f, 0:REACH, :]
         row_send[1, span, :] = vectors[f, high - REACH : high, :]
 
-    def row_copy(side):
+    def row_copy(side, channel):
+        span = slice(edges_at[channel], edges_at[channel + 1])
         return pltpu.make_async_remote_copy(
-            src_ref=row_send.at[side],
-            dst_ref=row_recv.at[1 - side, 0:sent, :],
-            send_sem=row_ss.at[side],
-            recv_sem=row_rs.at[1 - side],
+            src_ref=row_send.at[side, span, :],
+            dst_ref=row_recv.at[1 - side, span, :],
+            send_sem=row_ss.at[side, channel],
+            recv_sem=row_rs.at[1 - side, channel],
             device_id=(my_row - 1 + 2 * side, my_col),
             device_id_type=MESH,
         )
@@ -245,8 +259,9 @@
         )
 
     pl.semaphore_wait(barrier, rows + cols - 2)
-    for side in (0, 1):
-        pl.when(has[side])(lambda side=side: row_copy(side).start())
+    for channel in range(CHANNELS - 1):
+        for side in (0, 1):
+            pl.when(has[side])(lambda side=side, channel=channel: row_copy(side, channel).start())
 
     lane = lax.broadcasted_iota(jnp.int32, (high, LANES), 1)
     per = LANES // SLOT
@@ -314,6 +329,8 @@
         pl.when(beside[side])(lambda side=side: col_copy(1 - side).wait_recv())
     for side in (0, 1):
         pl.when(has[side])(lambda side=side: corner_copy(side).start())
+    for side in (0, 1):
+        pl.when(has[side])(lambda side=side: row_copy(side, CHANNELS - 1).start())
 
     def unpacked(left, right, f):
         p = f % per
@@ -338,19 +355,24 @@
     weight_total = sum(w * w for w in weights)
     offset_total = sum(r * w * w for r, w in zip(ratios, weights))
 
+    def cohere(channel, chunk):
+        block = pl.ds(pl.multiple_of(chunk * 8, 8), 8)
+        power1, power2, cross_re, cross_im = [
+            window(sums[4 * channel + i, block, :], 1) for i in range(4)
+        ]
+        scale = lax.rsqrt(power1 * power2 + EPSILON)
+        real = cross_re * scale
+        imag = cross_im * scale
+        found = (real * weights[channel], imag * weights[channel], real * real + imag * imag)
+        for i, value in enumerate(found):
+            if channel == 0:
+                mixed[i, block, :] = value
+            else:
+                mixed[i, block, :] += value
+
     def fit(chunk):
         block = pl.ds(pl.multiple_of(chunk * 8, 8), 8)
-        found = None
-        for k in range(CHANNELS):
-            power1, power2, cross_re, cross_im = [
-                window(sums[4 * k + i, block, :], 1) for i in range(4)
-            ]
-            scale = lax.rsqrt(power1 * power2 + EPSILON)
-            real = cross_re * scale
-            imag = cross_im * scale
-            parts = (real * weights[k], imag * weights[k], real * real + imag * imag)
-            found = parts if k == 0 else [a + b for a, b in zip(found, parts)]
-        weighted_re, weighted_im, confidence = [turn(a, RADIUS, 1) for a in found]
+        weighted_re, weighted_im, confidence = [turn(mixed[i, block, :], RADIUS, 1) for i in range(3)]
         phase, atten = gauss_newton(
             guess[1, block, :], guess[2, block, :], [first_fit[i, block, :] for i in range(5)],
             weighted_re, weighted_im, weight_total, offset_total,
@@ -373,17 +395,13 @@
     edge_chunks = SLOT // 8
 
     def middle(chunk, carry):
+        for channel in range(CHANNELS):
+            cohere(channel, chunk)
         fit(chunk)
         return carry
 
     lax.fori_loop(0, chunks, guessed, 0)
     lax.fori_loop(edge_chunks, chunks - edge_chunks, middle, 0)
-
-    for side in (0, 1):
-        @pl.when(has[side])
-        def _(side=side):
-            row_copy(1 - side).wait_recv()
-            corner_copy(1 - side).wait_recv()
 
     line = lax.broadcasted_iota(jnp.int32, (SLOT, LANES), 0)
     keep = (line < REACH, line >= SLOT - REACH)
@@ -402,36 +420,53 @@
 
     def halo_rows(side, f, strip):
         if strip < wide // LANES:
-            begin = first_row + f * REACH - side * (SLOT - REACH)
+            begin = row_begin(f) - side * (SLOT - REACH)
             value = row_recv[side, begin : begin + SLOT, strip * LANES : (strip + 1) * LANES]
         else:
             value = turn(corner(side, f), (1 - 2 * side) * (REACH - SLOT), 0)
         return jnp.where(keep[side], value, 0.0)
 
-    for side in (0, 1):
-        begin = side * (tall - SLOT)
-        for channel in range(CHANNELS):
+    def edge_chunk(step):
+        return step + step // edge_chunks * (chunks - 2 * edge_chunks)
+
+    for channel in range(CHANNELS):
+        for side in (0, 1):
+            @pl.when(has[side])
+            def _(side=side, channel=channel):
+                row_copy(1 - side, channel).wait_recv()
+                if channel == 0:
+                    corner_copy(1 - side).wait_recv()
+
+        for side in (0, 1):
+            begin = side * (tall - SLOT)
             for strip in range(full // LANES):
                 piece = slice(strip * LANES, (strip + 1) * LANES)
                 raws = [halo_rows(side, CHANNELS * i + channel, strip) for i in range(4)]
                 for i, product in enumerate(products(raws)):
                     sums[4 * channel + i, begin : begin + SLOT, piece] += running(product, side == 1)
-    for g in range(GUESS):
-        span = slice(g * GHOST, (g + 1) * GHOST)
-        guess[g, 0:GHOST, 0:wide] = row_recv[0, span, :]
-        guess[g, GHOST + high : tall, 0:wide] = row_recv[1, span, :]
-        guess[g, 0:GHOST, wide:full] = corner(0, RAW + g)[SLOT - GHOST :, :]
-        guess[g, GHOST + high : tall, wide:full] = corner(1, RAW + g)[0:GHOST, :]
-
-    ghosts = [
-        jnp.concatenate([guess[g, 0:GHOST, :], guess[g, GHOST + high : tall, :]], axis=0) for g in (1, 2)
-    ]
-    for i, moment in enumerate(volume_moments(*ghosts)):
-        first_fit[i, 0:GHOST, :] = moment[0:GHOST, :]
-        first_fit[i, GHOST + high : tall, :] = moment[GHOST : 2 * GHOST, :]
+
+        def edge_cohere(step, carry, channel=channel):
+            cohere(channel, edge_chunk(step))
+            return carry
+
+        lax.fori_loop(0, 2 * edge_chunks, edge_cohere, 0)
+        if channel == 0:
+            for g in range(GUESS):
+                span = guess_rows(g)
+                guess[g, 0:GHOST, 0:wide] = row_recv[0, span, :]
+                guess[g, GHOST + high : tall, 0:wide] = row_recv[1, span, :]
+                guess[g, 0:GHOST, wide:full] = corner(0, RAW + g)[SLOT - GHOST :, :]
+                guess[g, GHOST + high : tall, wide:full] = corner(1, RAW + g)[0:GHOST, :]
+
+            ghosts = [
+                jnp.concatenate([guess[g, 0:GHOST, :], guess[g, GHOST + high : tall, :]], axis=0) for g in (1, 2)
+            ]
+            for i, moment in enumerate(volume_moments(*ghosts)):
+                first_fit[i, 0:GHOST, :] = moment[0:GHOST, :]
+                first_fit[i, GHOST + high : tall, :] = moment[GHOST : 2 * GHOST, :]
 
     def edges(step, carry):
-        fit(step + step // edge_chunks * (chunks - 2 * edge_chunks))
+        fit(edge_chunk(step))
         return carry
 
     lax.fori_loop(0, 2 * edge_chunks, edges, 0)
@@ -461,8 +496,11 @@
     parts[0] = start[GHOST : GHOST + high, 0:wide]
     for i in range(ITERS):
         parts[1 + i] = basis[i][GHOST : GHOST + high, 0:wide]
-    parts[1 + ITERS] = start_buf[1, GHOST : GHOST + high, 0:wide]
-    store = pltpu.make_async_copy(parts, parts_out, store_sem)
+    results[1] = start_buf[1, GHOST : GHOST + high, 0:wide]
+
+    def store(i):
+        return pltpu.make_async_copy(results.at[i], parts_out.at[i], store_sem.at[i])
+
     own = inside & (row_at >= 0) & (row_at < high) & (lane_at < wide)
     for m in range(2 * ITERS):
         product = jnp.where(own, basis[m // 2] * basis[m - m // 2], 0.0)
@@ -496,7 +534,7 @@
 
     for k in range(1, rows):
         row_share(k).start()
-    store.start()
+    store(1).start()
     row_part[my_row] = mine[...]
     for k in range(1, rows):
         row_arrival(k).wait_recv()
@@ -525,20 +563,24 @@
     everything = jnp.sum(everything, axis=1, keepdims=True)
     moments = [everything[m : m + 1, :] for m in range(2 * ITERS)]
     answer = solve_coefficients(moments)
+    result = parts[0]
     for i, scale in enumerate(answer):
-        answer_out[i : i + 1, :] = jnp.broadcast_to(scale, (1, wide))
-    answer_out[ITERS:, :] = jnp.zeros((8 - ITERS, wide), jnp.float32)
-    store.wait()
+        result = result + scale * parts[1 + i]
+    results[0] = result
+    store(0).start()
 
     for side in (0, 1):
         @pl.when(has[side])
         def _(side=side):
-            row_copy(side).wait_send()
+            for channel in range(CHANNELS):
+                row_copy(side, channel).wait_send()
             corner_copy(side).wait_send()
 
         pl.when(beside[side])(lambda side=side: col_copy(side).wait_send())
     for k in range(1, rows):
         row_share(k).wait_send()
+    for i in (0, 1):
+        store(i).wait()
     for k in range(1, cols):
         col_share(k, my_col).wait_send()
 
@@ -549,20 +591,20 @@
     vectors = scatter_vectors.reshape(RAW, high, wide)
     full = wide + LANES
     tall = high + 2 * GHOST
-    edge = -(-(RAW * REACH + GUESS * GHOST) // 8) * 8
+    edges_at = [0]
+    for channel in range(CHANNELS):
+        held = 4 * REACH + (GUESS * GHOST if channel == 0 else 0)
+        edges_at.append(edges_at[-1] + -(-held // 8) * 8)
+    edge = edges_at[-1]
     packed = -(-(RAW + GUESS) * SLOT // LANES) * LANES
-    vmem = pl.BlockSpec(memory_space=pltpu.VMEM)
     f32 = jnp.float32
     dma = pltpu.SemaphoreType.DMA
-    out = (
-        jax.ShapeDtypeStruct((2 + ITERS, high, wide), f32),
-        jax.ShapeDtypeStruct((8, wide), f32),
-    )
-    parts, answer = pl.pallas_call(
-        functools.partial(kernel, counts),
+    out = jax.ShapeDtypeStruct((2, high, wide), f32)
+    results = pl.pallas_call(
+        functools.partial(kernel, counts, edges_at),
         out_shape=out,
         in_specs=[pl.BlockSpec(memory_space=pltpu.HBM)] * 5,
-        out_specs=(pl.BlockSpec(memory_space=pltpu.HBM), vmem),
+        out_specs=pl.BlockSpec(memory_space=pltpu.HBM),
         scratch_shapes=[
             pltpu.SMEM((CHANNELS,), f32),
             pltpu.VMEM((RAW, high, wide), f32),
@@ -570,11 +612,13 @@
             pltpu.VMEM((high, wide), f32),
             pltpu.VMEM((high, wide), f32),
             dma((5,)),
-            dma(()),
-            pltpu.VMEM((2 + ITERS, high, wide), f32),
+            dma((2,)),
+            pltpu.VMEM((2, high, wide), f32),
+            pltpu.VMEM((3, tall, full), f32),
+            pltpu.VMEM((1 + ITERS, high, wide), f32),
             pltpu.VMEM((5, tall, full), f32),
             pltpu.VMEM((2, edge, wide), f32),
-            pltpu.VMEM((2, edge + 8, wide), f32),
+            pltpu.VMEM((2, edge, wide), f32),
             pltpu.VMEM((2, high, packed), f32),
             pltpu.VMEM((2, high, packed), f32),
             pltpu.VMEM((2, 2, SLOT, packed), f32),
@@ -585,7 +629,7 @@
             pltpu.VMEM((8, LANES), f32),
             pltpu.VMEM((rows, 8, LANES), f32),
             pltpu.VMEM((cols, 8, LANES), f32),
-            dma((2,)), dma((2,)), dma((2,)), dma((2,)), dma((2,)), dma((2,)),
+            dma((2, CHANNELS)), dma((2, CHANNELS)), dma((2,)), dma((2,)), dma((2,)), dma((2,)),
             dma((rows,)), dma((rows,)), dma((cols,)), dma((cols,)),
         ],
         compiler_params=pltpu.CompilerParams(
@@ -595,10 +639,7 @@
             flops=2000 * high * wide, bytes_accessed=80 * high * wide, transcendentals=8 * high * wide
         ),
     )(ground_ratio, vectors, vertical_wavenumber, initial_phase, initial_extinction)
-    heights = parts[0]
-    for i in range(ITERS):
-        heights = heights + answer[i : i + 1, :] * parts[1 + i]
-    return (heights, parts[1 + ITERS])
+    return (results[0], results[1])
 
 
 def solution(mesh):

time: 28.6 us -> 26.6 us (0.930)
  other arithmetic: 1.59 us -> 0 us
  local copies, waits for them, and re-layouts: 2.31 us -> 1.53 us
  Pallas kernels: 23.7 us -> 24.3 us
    add x1 -> x0, other arithmetic: 1.59 us -> none  [local(): heights = heights + answer[i:i + 1, :] * parts[1 + i]]
    slice x1 -> x0, local copies, waits for them, and re-layouts: 0.84 us -> none  [local(): heights = heights + answer[i:i + 1, :] * parts[1 + i]]
    pallas_call x1, Pallas kernels: 23.7 us -> 24.3 us  [local(): pl.pallas_call(functools.partial(kernel, counts, edges_at), out_shape=out...]
where the time goes in v2:
time: 26.6 us; the launch traced here: 26.4 us
  Pallas kernels  24.3 us (91%)
  local copies, waits for them, and re-layouts  1.53 us (6%)
  between operations  0.64 us (2%)
    pallas_call x1, Pallas kernels, local(): pl.pallas_call(functools.partial(kernel, counts, edges_at), out_shape=out...  24.3 us
    squeeze x1, local copies, waits for them, and re-layouts, local(): return (results[0], results[1])  1.53 us

profile of v2, /device:TPU:0, one launch (start us, length us, event | category | flops | bytes accessed | tf_op | source)
XLA Modules:
  0.0 26.4 jit_solution(10699127879517432195)
XLA Ops:
  0.6 24.3 %shard_map.68 = f32[2,32,512]{2,1,0:T(8,128)} custom-call(f32[3]{0:T(128)} %ratio_in.1, f32[12,32,512]{2,1,0:T(8,128)} %bitcast.5, f32[32,512]{1,0:T(8,128)} %wavenumber_in.1, f32[32,512]{1,0:T(8,128)} %phase_in.1, f32[32,512]{1,0:T(8,128)} %atten_in.1), custom_call_target="tpu_custom_call" | custom-call | flops 32768000 | bytes 1310720 | tf_op jit(solution)/shard_map/pallas_call | solution.py:603
  24.9 1.5 %slice_bitcast_fusion = (f32[32,512]{1,0:T(8,128)}, f32[32,512]{1,0:T(8,128)}) fusion(f32[2,32,512]{2,1,0:T(8,128)} %shard_map.68), kind=kLoop, calls=%fused_computation | loop fusion | bytes 262144 | tf_op jit(solution)/shard_map/squeeze | solution.py:642

commit v3 on v2

--- a/solution.py
+++ b/solution.py
@@ -469,7 +469,7 @@
         fit(edge_chunk(step))
         return carry
 
-    lax.fori_loop(0, 2 * edge_chunks, edges, 0)
+    lax.fori_loop(0, 2 * edge_chunks, edges, 0, unroll=2)
 
     row_at = lax.broadcasted_iota(jnp.int32, (tall, full), 0) - GHOST
     lane_at = lax.broadcasted_iota(jnp.int32, (tall, full), 1)

time: 26.6 us -> 26.5 us (level)
  no operation moved by 1% of the time
where the time goes in v3:
time: 26.5 us; the launch traced here: 26.3 us
  Pallas kernels  24.1 us (91%)
  local copies, waits for them, and re-layouts  1.53 us (6%)
  between operations  0.64 us (2%)
    pallas_call x1, Pallas kernels, local(): pl.pallas_call(functools.partial(kernel, counts, edges_at), out_shape=out...  24.1 us
    squeeze x1, local copies, waits for them, and re-layouts, local(): return (results[0], results[1])  1.53 us

profile of v3, /device:TPU:0, one launch (start us, length us, event | category | flops | bytes accessed | tf_op | source)
XLA Modules:
  0.0 26.3 jit_solution(11047974234695800108)
XLA Ops:
  0.6 24.1 %shard_map.68 = f32[2,32,512]{2,1,0:T(8,128)} custom-call(f32[3]{0:T(128)} %ratio_in.1, f32[12,32,512]{2,1,0:T(8,128)} %bitcast.5, f32[32,512]{1,0:T(8,128)} %wavenumber_in.1, f32[32,512]{1,0:T(8,128)} %phase_in.1, f32[32,512]{1,0:T(8,128)} %atten_in.1), custom_call_target="tpu_custom_call" | custom-call | flops 32768000 | bytes 1310720 | tf_op jit(solution)/shard_map/pallas_call | solution.py:603
  24.8 1.5 %slice_bitcast_fusion = (f32[32,512]{1,0:T(8,128)}, f32[32,512]{1,0:T(8,128)}) fusion(f32[2,32,512]{2,1,0:T(8,128)} %shard_map.68), kind=kLoop, calls=%fused_computation | loop fusion | bytes 262144 | tf_op jit(solution)/shard_map/squeeze | solution.py:642

commit v4 on v3

--- a/solution.py
+++ b/solution.py
@@ -258,11 +258,6 @@
             device_id_type=MESH,
         )
 
-    pl.semaphore_wait(barrier, rows + cols - 2)
-    for channel in range(CHANNELS - 1):
-        for side in (0, 1):
-            pl.when(has[side])(lambda side=side, channel=channel: row_copy(side, channel).start())
-
     lane = lax.broadcasted_iota(jnp.int32, (high, LANES), 1)
     per = LANES // SLOT
     packs = (RAW + GUESS + per - 1) // per
@@ -284,8 +279,13 @@
         col_send[0, :, k * LANES : (k + 1) * LANES] = low
         col_send[1, :, k * LANES : (k + 1) * LANES] = top
 
+    pl.semaphore_wait(barrier, rows + cols - 2)
     for side in (0, 1):
         pl.when(beside[side])(lambda side=side: col_copy(side).start())
+    for channel in range(CHANNELS - 1):
+        for side in (0, 1):
+            pl.when(has[side])(lambda side=side, channel=channel: row_copy(side, channel).start())
+
 
     for side in (0, 1):
         @pl.when(jnp.logical_not(has[side]))

time: 26.5 us -> 26.4 us (level)
  no operation moved by 1% of the time
where the time goes in v4:
time: 26.4 us; the launch traced here: 26.2 us
  Pallas kernels  24 us (91%)
  local copies, waits for them, and re-layouts  1.53 us (6%)
  between operations  0.64 us (2%)
    pallas_call x1, Pallas kernels, local(): pl.pallas_call(functools.partial(kernel, counts, edges_at), out_shape=out...  24 us
    squeeze x1, local copies, waits for them, and re-layouts, local(): return (results[0], results[1])  1.53 us

profile of v4, /device:TPU:0, one launch (start us, length us, event | category | flops | bytes accessed | tf_op | source)
XLA Modules:
  0.0 26.2 jit_solution(6172978537054657259)
XLA Ops:
  0.6 24.0 %shard_map.68 = f32[2,32,512]{2,1,0:T(8,128)} custom-call(f32[3]{0:T(128)} %ratio_in.1, f32[12,32,512]{2,1,0:T(8,128)} %bitcast.5, f32[32,512]{1,0:T(8,128)} %wavenumber_in.1, f32[32,512]{1,0:T(8,128)} %phase_in.1, f32[32,512]{1,0:T(8,128)} %atten_in.1), custom_call_target="tpu_custom_call" | custom-call | flops 32768000 | bytes 1310720 | tf_op jit(solution)/shard_map/pallas_call | solution.py:603
  24.7 1.5 %slice_bitcast_fusion = (f32[32,512]{1,0:T(8,128)}, f32[32,512]{1,0:T(8,128)}) fusion(f32[2,32,512]{2,1,0:T(8,128)} %shard_map.68), kind=kLoop, calls=%fused_computation | loop fusion | bytes 262144 | tf_op jit(solution)/shard_map/squeeze | solution.py:642
